TPU v7x, 1024 devices: a whole 4x8x16 slice. The times are simulated.
1024 devices in a mesh: gx: 8 (over y), gy: 4 (over x), gz: 32 (over z, core).
Axes of the slice: x: 4, y: 8, z: 16, core: 2. Of those that a mesh axis runs over, the one named last changes fastest.
Arguments:
- tokens: bfloat16 [512, 10240], P('gy', ('gx', 'gz')), may hold values from -6 to 6
- w_up: bfloat16 [10240, 15872], P('gx', ('gz', 'gy')), may hold values from -0.0625 to 0.0625
- w_down: bfloat16 [15872, 10240], P(('gz', 'gy'), 'gx'), may hold values from -0.046875 to 0.046875
- out_grad: bfloat16 [512, 10240], P('gy', ('gx', 'gz')), may hold values from -6 to 6
Outputs:
- output: bfloat16 [512, 10240], P('gy', ('gx', 'gz'))
- grad_tokens: bfloat16 [512, 10240], P('gy', ('gx', 'gz'))
- grad_up: bfloat16 [10240, 15872], P('gx', ('gz', 'gy'))
- grad_down: bfloat16 [15872, 10240], P(('gz', 'gy'), 'gx')
All inputs are finite; a program needn't handle non-finite values.
Results may differ from a plain program's by a relative error of at most 0.0049.
Values may be sent and summed in bfloat16 or wider, within the bound.
A program may use at most 32 MiB of HBM per device.

v0:
```python
import math

import jax
import jax.numpy as jnp
from jax import lax
from jax.sharding import PartitionSpec as P


def gelu_parts(pre):
    cdf = 0.5 * (1.0 + jax.scipy.special.erf(pre / math.sqrt(2.0)))
    dens = jnp.exp(-0.5 * pre * pre) / math.sqrt(2.0 * math.pi)
    return (pre * cdf, cdf + pre * dens)


def contract_first(left, right):
    return lax.dot_general(
        left, right, (((0,), (0,)), ((), ())), preferred_element_type=jnp.float32
    )


def contract_last(left, right):
    return lax.dot_general(
        left, right, (((1,), (1,)), ((), ())), preferred_element_type=jnp.float32
    )


def local(tokens, w_up, w_down, out_grad):
    panel, grad_panel = (
        lax.all_gather(tokens, "gz", axis=1, tiled=True),
        lax.all_gather(out_grad, "gz", axis=1, tiled=True),
    )
    up_panel, down_panel = (
        lax.all_gather(w_up, "gy", axis=1, tiled=True),
        lax.all_gather(w_down, "gy", axis=0, tiled=True),
    )
    pre_part = jnp.dot(panel, up_panel, preferred_element_type=jnp.float32)
    pre_share = lax.psum_scatter(pre_part, "gx", scatter_dimension=1, tiled=True)
    value, slope = gelu_parts(pre_share)
    hidden = lax.all_gather(value.astype(jnp.bfloat16), "gx", axis=1, tiled=True)
    out_part = jnp.dot(hidden, down_panel, preferred_element_type=jnp.float32)
    output = lax.psum_scatter(out_part, "gz", scatter_dimension=1, tiled=True).astype(jnp.bfloat16)
    hidden_part = contract_last(grad_panel, down_panel)
    hidden_share = lax.psum_scatter(hidden_part, "gx", scatter_dimension=1, tiled=True)
    grad_pre = lax.all_gather((hidden_share * slope).astype(jnp.bfloat16), "gx", axis=1, tiled=True)
    input_part = contract_last(grad_pre, up_panel)
    grad_tokens = lax.psum_scatter(input_part, "gz", scatter_dimension=1, tiled=True).astype(
        jnp.bfloat16
    )
    token_rows, cotan_rows = (
        lax.all_gather(panel, "gy", axis=0, tiled=True),
        lax.all_gather(grad_panel, "gy", axis=0, tiled=True),
    )
    hidden_cols, grad_cols = (
        lax.all_to_all(hidden, "gy", split_axis=1, concat_axis=0, tiled=True),
        lax.all_to_all(grad_pre, "gy", split_axis=1, concat_axis=0, tiled=True),
    )
    grad_up = contract_first(token_rows, grad_cols)
    grad_down = contract_first(hidden_cols, cotan_rows)
    return (output, grad_tokens, grad_up.astype(jnp.bfloat16), grad_down.astype(jnp.bfloat16))


def solution(mesh):
    placed = (
        P("gy", ("gx", "gz")),
        P("gx", ("gz", "gy")),
        P(("gz", "gy"), "gx"),
        P("gy", ("gx", "gz")),
    )
    return jax.shard_map(
        local,
        mesh=mesh,
        in_specs=placed,
        out_specs=(
            P("gy", ("gx", "gz")),
            P("gy", ("gx", "gz")),
            P("gx", ("gz", "gy")),
            P(("gz", "gy"), "gx"),
        ),
        check_vma=False,
    )
```

profile of v0, /device:TPU:1, one launch (start us, length us, event | category | flops | bytes accessed | tf_op | source)
XLA Modules:
  0.0 414.7 jit_solution(9681611891491580243)
XLA Ops:
  7.2 1.9 copy.13
  10.0 48.0 %all_gather.24 = bf16[128,1280]{0,1:T(8,128)(2,1)} all-gather(bf16[128,40]{0,1:T(8,128)(2,1)S(1)} %copy-done.2), channel_id=1, replica_groups=mesh['gx'=8,'gy'=4,'gz'=32] {'gz'}, dimensions={1}, use_global_device_ids=true | all-gather | bytes 337920 | tf_op jit(solution)/shard_map/all_gather | solution.py:29
  58.0 30.6 %all_gather.28 = bf16[128,1280]{0,1:T(8,128)(2,1)} all-gather(bf16[128,40]{0,1:T(8,128)(2,1)S(1)} %copy-done.3), channel_id=1, replica_groups=mesh['gx'=8,'gy'=4,'gz'=32] {'gz'}, dimensions={1}, use_global_device_ids=true | all-gather | bytes 337920 | tf_op jit(solution)/shard_map/all_gather | solution.py:30
  88.8 1.5 reshape.15
  90.2 3.5 all-gather.15.cloned.1.call-done
  93.7 1.4 reshape.19
  96.6 17.7 %fusion.11 = (f32[128,64]{0,1:T(8,128)S(1)}, f32[128,64]{0,1:T(8,128)S(1)}) fusion(f32[128,496]{0,1:T(8,128)S(1)} %fusion.14, f32[128,496]{0,1:T(8,128)S(1)} %fusion.15), kind=kCustom, calls=%all-reduce-scatter.2 | all-reduce-scatter fusion | flops 131073 | bytes 577536
  114.4 1.5 collective-permute-start.1
  115.9 2.1 collective-permute-start
  118.0 1.3 dynamic-slice.10
  120.4 21.0 %all-gather.3 = bf16[8,62,128]{2,1,0:T(8,128)(2,1)S(1)} all-gather(bf16[1,62,128]{2,1,0:T(8,128)(2,1)S(1)} %get-tuple-element.20), channel_id=1, replica_groups=mesh['gx'=8,'gy'=4,'gz'=32] {'gx'}, dimensions={0}, use_global_device_ids=true | all-gather | bytes 142848 | tf_op jit(solution)/shard_map/all_gather | solution.py:44
  141.5 1.5 fusion.13
  143.0 18.8 %all-gather.1 = bf16[8,62,128]{2,1,0:T(8,128)(2,1)S(1)} all-gather(bf16[1,62,128]{2,1,0:T(8,128)(2,1)S(1)} %get-tuple-element.21), channel_id=1, replica_groups=mesh['gx'=8,'gy'=4,'gz'=32] {'gx'}, dimensions={0}, use_global_device_ids=true | all-gather | bytes 142848 | tf_op jit(solution)/shard_map/all_gather | solution.py:39
  161.9 1.5 fusion.12
  164.1 3.3 all-to-all-start
  168.1 5.2 %all-to-all-done = bf16[128,4,124]{0,2,1:T(8,128)(2,1)S(1)} async-done(((bf16[128,4,124]{0,2,1:T(8,128)(2,1)}), bf16[128,4,124]{0,2,1:T(8,128)(2,1)S(1)}, u32[]{:S(2)}, u32[]{:S(2)}) %all-to-all-start) | async-done | bytes 127008 | tf_op jit(solution)/shard_map/all_to_all | solution.py:55
  173.3 3.3 all-to-all-start.1
  176.8 1.9 fusion.2
  179.6 1.8 all-to-all-done.1
  181.6 2.6 convolution_convert_fusion
  184.2 110.0 %reduce-scatter.13.cloned.1.call-done = f32[128,40]{0,1:T(8,128)} async-done(((f32[128,1280]{0,1:T(8,128)}), f32[128,40]{0,1:T(8,128)}) %reduce-scatter.13.cloned.1.call-update) | async-done | bytes 20496
  294.2 1.3 convert_element_type.24
  295.5 111.0 %reduce-scatter.11.cloned.1.call-done = f32[128,40]{0,1:T(8,128)} async-done(((f32[128,1280]{0,1:T(8,128)}), f32[128,40]{0,1:T(8,128)}) %reduce-scatter.11.cloned.1.call-update) | async-done | bytes 20496
  406.5 1.3 convert_element_type.22
  (39 shorter events, 5.6 us)
Async XLA Ops:
  7.2 2.8 copy-start.2
  7.2 50.8 %copy-start.3 = (bf16[128,40]{0,1:T(8,128)(2,1)S(1)}, bf16[128,40]{0,1:T(8,128)(2,1)}, u32[]{:S(2)}) copy-start(bf16[128,40]{0,1:T(8,128)(2,1)} %param.7) | copy-start | bytes 30724
  7.2 81.6 %all-gather.13.cloned.1.call-start = ((), (), s32[]{:S(2)}) async-start(), calls=%async_computation.6 | async-start | bytes 1638400 | tf_op jit(solution)/shard_map/all_gather | solution.py:33
  9.2 84.6 %all-gather.15.cloned.1.call-start = ((), (), s32[]{:S(2)}) async-start(), calls=%async_computation.7 | async-start | bytes 1638400 | tf_op jit(solution)/shard_map/all_gather | solution.py:34
  9.9 166.9 %all-gather.9.cloned.1.call-start = ((), (), s32[]{:S(2)}) async-start(), calls=%async_computation.4 | async-start | bytes 1638400 | tf_op jit(solution)/shard_map/all_gather | solution.py:50
  57.9 123.6 %all-gather.11.cloned.1.call-start = ((), (), s32[]{:S(2)}) async-start(), calls=%async_computation.5 | async-start | bytes 1638400 | tf_op jit(solution)/shard_map/all_gather | solution.py:51
  88.7 205.5 %reduce-scatter.13.cloned.1.call-start = ((), (), s32[]{:S(2)}) async-start(), calls=%async_computation.9 | async-start | bytes 675840
  90.2 4.9 %copy-start.1 = (bf16[128,1280]{0,1:T(8,128)(2,1)S(1)}, bf16[128,1280]{0,1:T(8,128)(2,1)}, u32[]{:S(2)}) copy-start(bf16[128,1280]{0,1:T(8,128)(2,1)} %all_gather.24) | copy-start | bytes 983044
  95.2 1.0 copy-start
  114.4 5.6 %collective-permute-start.1 = (f32[128,14]{0,1:T(8,128)S(1)}, f32[128,14]{0,1:T(8,128)S(1)}, u32[]{:S(2)}, u32[]{:S(2)}) collective-permute-start(f32[128,14]{0,1:T(8,128)S(1)} %slice.1), channel_id=1, source_target_pairs={{0,128},{128,256},{256,384},{384,512},{512,640},{640,768},{768,896... | collective-permute-start | bytes 21512
  115.9 4.2 %collective-permute-start = (f32[128,14]{0,1:T(8,128)S(1)}, f32[128,14]{0,1:T(8,128)S(1)}, u32[]{:S(2)}, u32[]{:S(2)}) collective-permute-start(f32[128,14]{0,1:T(8,128)S(1)} %slice), channel_id=1, source_target_pairs={{0,128},{128,256},{256,384},{384,512},{512,640},{640,768},{768,896... | collective-permute-start | bytes 21512
  143.0 263.5 %reduce-scatter.11.cloned.1.call-start = ((), (), s32[]{:S(2)}) async-start(), calls=%async_computation.8 | async-start | bytes 675840
  164.1 9.2 %all-to-all-start = ((bf16[128,4,124]{0,2,1:T(8,128)(2,1)}), bf16[128,4,124]{0,2,1:T(8,128)(2,1)S(1)}, u32[]{:S(2)}, u32[]{:S(2)}) async-start(bf16[128,4,124]{0,2,1:T(8,128)(2,1)} %all_to_all.28), calls=%async_computation | async-start | bytes 262144 | tf_op jit(solution)/shard_map/all_to_all | solution.py:55
  173.3 8.1 %all-to-all-start.1 = ((bf16[128,4,124]{0,2,1:T(8,128)(2,1)}), bf16[128,4,124]{0,2,1:T(8,128)(2,1)S(1)}, u32[]{:S(2)}, u32[]{:S(2)}) async-start(bf16[128,4,124]{0,2,1:T(8,128)(2,1)} %all_to_all.32), calls=%async_computation.1 | async-start | bytes 262144 | tf_op jit(solution)/shard_map/all_to_all | solution.py:54
Sparse Core Ops, SparseCore 0:
  11.3 43.2 all-gather.12
  57.3 36.3 all-gather.14
  96.4 39.4 all-gather.8
  138.5 40.5 all-gather.10
  182.3 111.8 reduce-scatter.12
  297.8 108.6 reduce-scatter.10
where the time goes:
time: 418 us; the launch traced here: 415 us
  waiting for transfers between devices  232 us (56%)
  blocking collectives  136 us (33%)
  between operations  15 us (4%)
  starting transfers between devices  10.5 us (3%)
  local copies, waits for them, and re-layouts  9.6 us (2%)
  matrix products  8.45 us (2%)
    unnamed x10, waiting for transfers between devices  222 us
    all_gather x1, blocking collectives, local(): lax.all_gather(tokens, 'gz', axis=1, tiled=True)  48 us
    all_gather x1, blocking collectives, local(): lax.all_gather(out_grad, 'gz', axis=1, tiled=True)  30.6 us
    all_gather x1, blocking collectives, local(): lax.all_gather((hidden_share * slope).astype(jnp.bfloat16), 'gx', axis=1,...  21 us
    all_gather x1, blocking collectives, local(): lax.all_gather(value.astype(jnp.bfloat16), 'gx', axis=1, tiled=True)  18.8 us
    unnamed x1, blocking collectives  17.7 us
  transfers between devices with their start and end apart: 10, of which 5 were waited for; matrix products, arithmetic and copies ran while one was open for 8% of the time, Pallas kernels for 0%

commit v1 on v0

v1 whole, which is shorter than its diff:
```python
import functools
import math

import jax
import jax.numpy as jnp
from jax import lax
from jax.experimental import pallas as pl
from jax.experimental.pallas import tpu as pltpu
from jax.sharding import PartitionSpec as P

MESH = pl.DeviceIdType.MESH
BF16, F32 = jnp.bfloat16, jnp.float32
LANES = 128


def dot(left, right, dims=((1,), (0,))):
    return lax.dot_general(left, right, (dims, ((), ())), preferred_element_type=F32)


def kernel(sizes, *refs):
    nx, ny, nz, rows, half, fcols = sizes
    (tok, cot, w_up, w_dn, o_out, o_gt, o_gu, o_gd,
     tile, pair_in, own_f, pad_out, xt, w, wt, give_up, give_dn,
     part_f, part_b, got_b, share, other, ht,
     send_c, got_x, own_c, send_z, got_z, final, out_give, out_got,
     g_give_up, g_give_dn, g_got_up, g_got_dn,
     s_pair, r_pair, s_az, r_az, s_ax, r_ax, s_b, r_b, s_h, r_h, s_cx, r_cx, s_cz, r_cz) = refs
    y, x = lax.axis_index("gx"), lax.axis_index("gy")
    g = lax.axis_index("gz")
    z, c = lax.div(g, 2), lax.rem(g, 2)
    width = xt.shape[0]
    tokens = xt.shape[1]
    hid = ht.shape[0]
    hrows = hid // ny

    def dev(yy, xx, zz, cc):
        return (yy, xx, zz * 2 + cc)

    partner = dev(y, x, z, 1 - c)

    def at_x(k):
        return dev(y, lax.rem(x + k, nx), z, c)

    def at_y(k):
        return dev(lax.rem(y + k, ny), x, z, c)

    def at_z(k):
        return dev(y, x, lax.rem(z + k, nz), c)

    def remote(src, dst, ssem, rsem, device):
        return pltpu.make_async_remote_copy(
            src_ref=src, dst_ref=dst, send_sem=ssem, recv_sem=rsem, device_id=device, device_id_type=MESH)

    def loop(n, body):
        def step(i, carry):
            body(i)
            return carry
        lax.fori_loop(0, n, step, 0)

    def far_first(i):
        m = lax.div(i + 1, 2)
        return nz // 2 + m * (2 * lax.rem(i + 1, 2) - 1)

    def rblock(i):
        return pl.ds(pl.multiple_of(i * rows, 16), rows)

    def lblock(i):
        return pl.ds(pl.multiple_of(i * LANES, LANES), LANES)

    barrier = pltpu.get_barrier_semaphore()

    def hello(device):
        pl.semaphore_signal(barrier, inc=1, device_id=device, device_id_type=MESH)

    hello(partner)
    loop(nz - 1, lambda i: hello(at_z(i + 1)))
    loop(nx - 1, lambda i: hello(at_x(i + 1)))
    loop(ny - 1, lambda i: hello(at_y(i + 1)))

    first = c == 0
    tile[...] = jnp.zeros_like(tile)
    tile[0, :, :half] = jnp.where(first, tok[...], cot[...])
    tile[1, :, :half] = jnp.where(first, cot[...], tok[...])
    pl.semaphore_wait(barrier, 1 + (nz - 1) + (nx - 1) + (ny - 1))
    to_pair = remote(tile.at[1], pair_in, s_pair.at[0], r_pair.at[0], partner)
    to_pair.start()
    mine = tile[0].astype(F32).T[:half]
    own_f[pl.ds(pl.multiple_of(c * half, 8), half), :] = mine
    to_pair.wait_recv()
    theirs = pair_in[...].astype(F32).T[:half]
    own_f[pl.ds(pl.multiple_of((1 - c) * half, 8), half), :] = theirs
    xt[rblock(z), lblock(x)] = own_f[...].astype(BF16)

    def block(zz):
        return xt.at[rblock(zz), lblock(x)]

    def over_z(i):
        k = far_first(i)
        return remote(block(z), block(z), s_az.at[k], r_az.at[z], at_z(k))

    def over_x(k, zz):
        return remote(block(zz), block(zz), s_ax.at[k, zz], r_ax.at[k, zz], at_x(k))

    loop(nz - 1, lambda i: over_z(i).start())
    loop(nx - 1, lambda i: over_x(i + 1, z).start())

    @pl.when(first)
    def _():
        w[:, :LANES] = jnp.zeros((width, LANES), BF16)
        w[:, :fcols] = w_up[...]
        give_dn[...] = jnp.zeros_like(give_dn)
        give_dn[:fcols, :] = w_dn[...]
        remote(give_dn, wt.at[:LANES, :], s_pair.at[1], r_pair.at[1], partner).start()

    @pl.when(c == 1)
    def _():
        give_up[...] = jnp.zeros_like(give_up)
        give_up[:, :fcols] = w_up[...]
        remote(give_up, w.at[:, LANES:], s_pair.at[2], r_pair.at[2], partner).start()
        wt[LANES:, :] = jnp.zeros((LANES, width), BF16)
        wt[LANES:LANES + fcols, :] = w_dn[...]

    def hand_on(j):
        zz = nz - 1 - j

        @pl.when(zz != z)
        def _():
            remote(block(zz), block(zz), s_az.at[0], r_az.at[zz], at_x(1)).wait_recv()
            for k in range(1, nx):
                over_x(k, zz).start()

    @pl.when(first)
    def _():
        remote(give_up, w.at[:, LANES:], s_pair.at[1], r_pair.at[2], partner).wait_recv()

        def turn(i):
            tall = pl.ds(pl.multiple_of(i * LANES, LANES), LANES)
            wt[:, tall] = w[tall, :].T
        loop(width // LANES, turn)

    @pl.when(c == 1)
    def _():
        remote(give_dn, wt.at[:LANES, :], s_pair.at[2], r_pair.at[1], partner).wait_recv()

        def turn(i):
            tall = pl.ds(pl.multiple_of(i * LANES, LANES), LANES)
            w[tall, :] = wt[:, tall].T
        loop(width // LANES, turn)

    loop(nz, hand_on)

    def arrived(i):
        for k in range(1, nx):
            landing = xt.at[rblock(i), lblock(lax.rem(x + nx - k, nx))]
            remote(landing, landing, s_ax.at[k, i], r_ax.at[k, i], at_x(1)).wait_recv()
    loop(nz, arrived)

    def first_product(i):
        cols = pl.ds(pl.multiple_of(i * LANES, LANES), LANES)
        p = dot(wt[...], xt[:, cols])
        part_f[:, cols] = p
        part_b[:, cols] = p.astype(BF16)
    loop(tokens // LANES, first_product)

    def hblock(i):
        return pl.ds(pl.multiple_of(i * hrows, 16), hrows)

    def share_of(k):
        return remote(part_b.at[hblock(lax.rem(y + k, ny)), :], got_b.at[k], s_b.at[k], r_b.at[k], at_y(k))

    y_order = sorted(range(1, ny), key=lambda k: -min(k, ny - k))
    for k in y_order:
        share_of(k).start()
    total = part_f[hblock(y), :]
    for k in reversed(y_order):
        share_of(k).wait_recv()
        total = total + got_b[k].astype(F32)
    share[...] = total
    swap = remote(share, other, s_pair.at[3], r_pair.at[3], partner)
    swap.start()
    swap.wait_recv()
    pre = jnp.where(first, total, other[...])
    cdf = 0.5 * (1.0 + lax.erf(pre * (1.0 / math.sqrt(2.0))))
    dens = jnp.exp(-0.5 * pre * pre) * (1.0 / math.sqrt(2.0 * math.pi))
    made = jnp.where(first, other[...] * (cdf + pre * dens), pre * cdf)
    ht[hblock(y), :] = made.astype(BF16)

    def spread(k):
        return remote(ht.at[hblock(y), :], ht.at[hblock(y), :], s_h.at[k], r_h.at[k], at_y(k))

    for k in y_order:
        spread(k).start()
    for k in reversed(y_order):
        landing = ht.at[hblock(lax.rem(y + ny - k, ny)), :]
        remote(landing, landing, s_h.at[k], r_h.at[k], at_y(1)).wait_recv()

    def to_x(k, d):
        return remote(send_c.at[rblock(d), lblock(lax.rem(x + k, nx))], got_x.at[k, rblock(d), :],
                      s_cx.at[k, d], r_cx.at[k, d], at_x(k))

    def second_product(i):
        d = lax.rem(z + far_first(i), nz)
        p = dot(w[rblock(d), :], ht[...])
        own_c[rblock(d), :] = jnp.zeros((rows, LANES), F32)
        send_c[rblock(d), :] = p.astype(BF16)
        for k in range(nx):
            @pl.when(x == k)
            def _(k=k):
                own_c[rblock(d), :] = p[:, k * LANES:(k + 1) * LANES]
        for k in (2, 1, 3):
            to_x(k, d).start()
    loop(nz, second_product)

    step_rows = 2 * LANES

    @pl.when(first)
    def _():
        def grad(i):
            tall = pl.ds(pl.multiple_of(i * step_rows, step_rows), step_rows)
            p = dot(xt[tall, :], ht[...], ((1,), (1,))).astype(BF16)
            o_gu[tall, :] = p[:, :fcols]
            g_give_up[tall, :] = p[:, LANES:]
        loop(width // step_rows, grad)
        remote(g_give_up, g_got_up, s_pair.at[4], r_pair.at[4], partner).start()

    @pl.when(c == 1)
    def _():
        def grad(i):
            tall = pl.ds(pl.multiple_of(i * step_rows, step_rows), step_rows)
            p = dot(ht[...], xt[tall, :], ((1,), (1,))).astype(BF16)
            g_give_dn[:, tall] = p[:LANES, :]
            o_gd[:, tall] = p[LANES:LANES + fcols, :]
        loop(width // step_rows, grad)
        remote(g_give_dn, g_got_dn, s_pair.at[5], r_pair.at[5], partner).start()

    def to_z(k):
        d = lax.rem(z + k, nz)
        return remote(send_z.at[rblock(d), :], got_z.at[z], s_cz.at[k], r_cz.at[z], at_z(k))

    def add_x(d):
        total = own_c[rblock(d), :]
        for k in range(1, nx):
            to_x(k, d).wait_recv()
            total = total + got_x[k, rblock(d), :].astype(F32)
        return total

    def pass_on(i):
        k = far_first(i)
        d = lax.rem(z + k, nz)
        send_z[rblock(d), :] = add_x(d).astype(BF16)
        to_z(k).start()
    loop(nz - 1, pass_on)
    final[:rows, :] = add_x(z)

    def collect(i):
        s = lax.rem(z + far_first(nz - 2 - i), nz)
        remote(got_z.at[s], got_z.at[s], s_cz.at[1], r_cz.at[s], at_z(1)).wait_recv()
        final[:rows, :] += got_z[s].astype(F32)
    loop(nz - 1, collect)

    pad_out[...] = jnp.zeros_like(pad_out)
    pad_out[0, :half, :] = final[pl.ds(pl.multiple_of(c * half, 8), half), :]
    pad_out[1, :half, :] = final[pl.ds(pl.multiple_of((1 - c) * half, 8), half), :]
    out_give[...] = pad_out[1].T.astype(BF16)
    back = remote(out_give, out_got, s_pair.at[6], r_pair.at[6], partner)
    back.start()
    kept = pad_out[0].T.astype(BF16)[:, :half]

    @pl.when(first)
    def _():
        remote(g_give_dn, g_got_dn, s_pair.at[4], r_pair.at[5], partner).wait_recv()
        o_gd[...] = g_got_dn[:fcols, :]
        o_gt[...] = kept
        back.wait_recv()
        o_out[...] = out_got[:, :half]
        remote(give_dn, wt.at[:LANES, :], s_pair.at[1], r_pair.at[1], partner).wait_send()
        remote(g_give_up, g_got_up, s_pair.at[4], r_pair.at[4], partner).wait_send()

    @pl.when(c == 1)
    def _():
        remote(g_give_up, g_got_up, s_pair.at[5], r_pair.at[4], partner).wait_recv()
        o_gu[...] = g_got_up[:, :fcols]
        o_out[...] = kept
        back.wait_recv()
        o_gt[...] = out_got[:, :half]
        remote(give_up, w.at[:, LANES:], s_pair.at[2], r_pair.at[2], partner).wait_send()
        remote(g_give_dn, g_got_dn, s_pair.at[5], r_pair.at[5], partner).wait_send()

    to_pair.wait_send()
    swap.wait_send()
    back.wait_send()
    for k in y_order:
        share_of(k).wait_send()
        spread(k).wait_send()
    loop(nz - 1, lambda i: over_z(i).wait_send())
    loop(nz - 1, lambda i: to_z(far_first(i)).wait_send())

    def sent(i):
        for k in range(1, nx):
            over_x(k, i).wait_send()
            to_x(k, i).wait_send()
    loop(nz, sent)


def local(shape, tokens, w_up, w_down, out_grad):
    nx, ny, nz = shape["gy"], shape["gx"], shape["gz"] // 2
    half = tokens.shape[1]
    rows = 2 * half
    width, fcols = w_up.shape
    count = tokens.shape[0] * nx
    hid = 2 * LANES
    vmem, dma = pltpu.VMEM, pltpu.SemaphoreType.DMA
    scratch = [
        vmem((2, LANES, LANES), BF16), vmem((LANES, LANES), BF16), vmem((rows, LANES), F32),
        vmem((2, LANES, LANES), F32),
        vmem((width, count), BF16), vmem((width, hid), BF16), vmem((hid, width), BF16),
        vmem((width, LANES), BF16), vmem((LANES, width), BF16),
        vmem((hid, count), F32), vmem((hid, count), BF16), vmem((ny, hid // ny, count), BF16),
        vmem((hid // ny, count), F32), vmem((hid // ny, count), F32), vmem((hid, count), BF16),
        vmem((width, count), BF16), vmem((nx, width, LANES), BF16), vmem((width, LANES), F32),
        vmem((width, LANES), BF16), vmem((nz, rows, LANES), BF16), vmem((rows, LANES), F32),
        vmem((LANES, LANES), BF16), vmem((LANES, LANES), BF16),
        vmem((width, LANES), BF16), vmem((LANES, width), BF16),
        vmem((width, LANES), BF16), vmem((LANES, width), BF16),
        dma((7,)), dma((7,)), dma((nz,)), dma((nz,)), dma((nx, nz)), dma((nx, nz)),
        dma((ny,)), dma((ny,)), dma((ny,)), dma((ny,)),
        dma((nx, nz)), dma((nx, nz)), dma((nz,)), dma((nz,)),
    ]
    whole = pl.BlockSpec(memory_space=pltpu.VMEM)
    return pl.pallas_call(
        functools.partial(kernel, (nx, ny, nz, rows, half, fcols)),
        out_shape=(
            jax.ShapeDtypeStruct(tokens.shape, BF16), jax.ShapeDtypeStruct(tokens.shape, BF16),
            jax.ShapeDtypeStruct(w_up.shape, BF16), jax.ShapeDtypeStruct(w_down.shape, BF16)),
        in_specs=[whole] * 4,
        out_specs=(whole,) * 4,
        scratch_shapes=scratch,
        compiler_params=pltpu.CompilerParams(
            collective_id=0, has_side_effects=True, vmem_limit_bytes=48 * 1024 * 1024),
    )(tokens, out_grad, w_up, w_down)


def solution(mesh):
    tokens, up, down = P("gy", ("gx", "gz")), P("gx", ("gz", "gy")), P(("gz", "gy"), "gx")
    return jax.shard_map(
        functools.partial(local, dict(mesh.shape)),
        mesh=mesh,
        in_specs=(tokens, up, down, tokens),
        out_specs=(tokens, tokens, up, down),
        check_vma=False,
    )
```

time: 418 us -> 107 us (0.26)
  waiting for transfers between devices: 232 us -> 0 us
  blocking collectives: 136 us -> 0 us
  Pallas kernels: 0 us -> 101 us
  between operations: 15 us -> 0.66 us
  starting transfers between devices: 10.5 us -> 0 us
  matrix products: 8.45 us -> 0 us
    unnamed x10 -> x0, waiting for transfers between devices: 222 us -> none
    all_gather x4 -> x0, blocking collectives: 118 us -> none  [the longest x1 48 us: local(): lax.all_gather(tokens, 'gz', axis=1, tiled=True)]
    pallas_call x0 -> x1, Pallas kernels: none -> 101 us  [local(): pl.pallas_call(functools.partial(kernel, (nx, ny, nz, rows, half, fcols))...]
    unnamed x1 -> x0, blocking collectives: 17.7 us -> none
    dot_general x6 -> x0, matrix products: 8.45 us -> none  [the longest x2 4.49 us: contract_first(): lax.dot_general(left, right, (((0,), (0,)), ((), ())), preferred_element_...]
    all_to_all x2 -> x0, waiting for transfers between devices: 6.99 us -> none  [the longest x1 5.17 us: local(): lax.all_to_all(grad_pre, 'gy', split_axis=1, concat_axis=0, tiled=True)]
    all_to_all x2 -> x0, starting transfers between devices: 6.65 us -> none  [the longest x1 3.33 us: local(): lax.all_to_all(grad_pre, 'gy', split_axis=1, concat_axis=0, tiled=True)]
  transfers between devices with their start and end apart: 10 -> 0, of which waited for: 5 -> 0; matrix products, arithmetic and copies ran while one was open for 8% -> 0% of each run, Pallas kernels for 0% -> 0%
where the time goes in v1:
time: 107 us
  Pallas kernels  101 us (94%)
  local copies, waits for them, and re-layouts  5.7 us (5%)
    pallas_call x1, Pallas kernels, local(): pl.pallas_call(functools.partial(kernel, (nx, ny, nz, rows, half, fcols))...  101 us
    unnamed x10, local copies, waits for them, and re-layouts  4.34 us

profile of v1, /device:TPU:1, one launch (start us, length us, event | category | flops | bytes accessed | tf_op | source)
XLA Modules:
  0.0 106.9 jit_solution(1458425799554166661)
XLA Ops:
  0.6 0.0 copy-start.2
  0.6 0.8 copy.8.refs_0_
  1.5 0.0 copy-done.2
  1.5 0.1 copy.9.refs_1_
  1.6 0.0 copy-start
  1.6 1.0 copy-done
  2.6 0.0 copy-start.1
  2.6 1.0 copy-done.1
  3.5 100.6 %shard_map.75 = (bf16[128,40]{1,0:T(8,128)(2,1)S(1)}, bf16[128,40]{1,0:T(8,128)(2,1)S(1)}, bf16[1280,124]{1,0:T(8,128)(2,1)S(1)}, bf16[124,1280]{1,0:T(8,128)(2,1)S(1)}) custom-call(bf16[128,40]{1,0:T(8,128)(2,1)S(1)} %copy.8.refs_0_, bf16[128,40]{1,0:T(8,128)(2,1)S(1)} %copy.9.refs_1_, bf16[1280,124]{1,0:T(8,128)(2,1)S(1)} %copy-done, ...), custom_call_target="tpu_custom_call" | custom-call | tf_op jit(solution)/shard_map/pallas_call | solution.py:330
  104.1 0.7 copy.10
  104.8 0.7 copy.11
  105.5 0.7 copy.14
  106.2 0.7 copy.15
Async XLA Ops:
  0.6 0.8 copy-start.2
  1.6 1.0 copy-start
  2.6 1.0 copy-start.1

commit v2 on v1

v2 whole, which is shorter than its diff:
```python
import functools
import math

import jax
import jax.numpy as jnp
from jax import lax
from jax.experimental import pallas as pl
from jax.experimental.pallas import tpu as pltpu
from jax.sharding import PartitionSpec as P

MESH = pl.DeviceIdType.MESH
BF16, F32 = jnp.bfloat16, jnp.float32
LANES = 128


def dot(left, right, dims=((1,), (0,))):
    return lax.dot_general(left, right, (dims, ((), ())), preferred_element_type=F32)


def kernel(sizes, *refs):
    nx, ny, nz, rows, half, fcols = sizes
    (tok, cot, w_up, w_dn, o_out, o_gt, o_gu, o_gd,
     give, pair_in, own_f, xt, w, wt, give_up, give_dn,
     part_f, part_b, got_b, share, other, ht,
     send_c, got_x, own_c, send_z, got_z, final, out_give, out_got,
     g_give_up, g_give_dn, g_got_up, g_got_dn,
     s_pair, r_pair, s_far, r_far, s_near, r_near, s_ax, r_ax, s_swap, r_swap, s_b, r_b, s_h, r_h, s_cx, r_cx, s_cz, r_cz) = refs
    y, x = lax.axis_index("gx"), lax.axis_index("gy")
    g = lax.axis_index("gz")
    z, c = lax.div(g, 2), lax.rem(g, 2)
    width = xt.shape[0]
    tokens = xt.shape[1]
    hid = ht.shape[0]
    hrows = hid // ny

    def dev(yy, xx, zz, cc):
        return (yy, xx, zz * 2 + cc)

    partner = dev(y, x, z, 1 - c)

    def at_x(k):
        return dev(y, lax.rem(x + k, nx), z, c)

    def at_y(k):
        return dev(lax.rem(y + k, ny), x, z, c)

    def at_z(k):
        return dev(y, x, lax.rem(z + k, nz), c)

    def remote(src, dst, ssem, rsem, device):
        return pltpu.make_async_remote_copy(
            src_ref=src, dst_ref=dst, send_sem=ssem, recv_sem=rsem, device_id=device, device_id_type=MESH)

    def loop(n, body):
        def step(i, carry):
            body(i)
            return carry
        lax.fori_loop(0, n, step, 0)

    def far_first(i):
        m = lax.div(i + 1, 2)
        return nz // 2 + m * (2 * lax.rem(i + 1, 2) - 1)

    def rblock(i):
        return pl.ds(pl.multiple_of(i * rows, 16), rows)

    def lblock(i):
        return pl.ds(pl.multiple_of(i * LANES, LANES), LANES)

    barrier = pltpu.get_barrier_semaphore()

    def hello(device):
        pl.semaphore_signal(barrier, inc=1, device_id=device, device_id_type=MESH)

    loop(nz - 1, lambda i: hello(at_z(far_first(i))))
    for k in range(1, ny):
        hello(at_y(k))
    for k in range(1, nx):
        hello(at_x(k))
    hello(partner)

    first = c == 0
    give[...] = jnp.zeros_like(give)
    give[:half, :] = jnp.where(first, cot[...], tok[...])
    own_f[pl.ds(pl.multiple_of(c * half, 8), half), :] = jnp.where(first, tok[...], cot[...]).astype(F32)
    give_dn[...] = jnp.zeros_like(give_dn)
    give_up[...] = jnp.zeros_like(give_up)
    give_dn[:fcols, :] = w_dn[...]
    give_up[:, :fcols] = w_up[...]

    order = (0, 2, 1, 3)
    place = {k: at for at, k in enumerate(order)}
    to_pair = remote(give, pair_in, s_pair.at[0], r_pair.at[0], partner)
    far = (nz // 2, nz // 4, 3 * nz // 4, 0)
    near = (2 + (nz - 4) * c, 1 + (nz - 2) * c, nz - 1 - (nz - 2) * c)

    def back_by(k):
        return lax.rem(z + 2 * nz - k, nz)

    def block(zz, at=0):
        return xt.at[rblock(zz), at * LANES:(at + 1) * LANES]

    def over_far(q):
        return remote(block(z), block(z), s_far.at[q], r_far.at[q], at_z(far[q]))

    def over_near(q, j):
        zz = back_by(far[q])
        return remote(block(zz), block(zz), s_near.at[q, j], r_near.at[q, j], at_z(near[j]))

    def over_x(k, zz):
        return remote(block(zz), block(zz, place[(nx - k) % nx]), s_ax.at[k, zz], r_ax.at[k, zz], at_x(k))

    def send_over_x(zz):
        for k in (2, 1, 3):
            over_x(k, zz).start()

    pl.semaphore_wait(barrier, 1 + (nz - 1) + (nx - 1) + (ny - 1))
    to_pair.start()
    to_pair.wait_recv()
    own_f[pl.ds(pl.multiple_of((1 - c) * half, 8), half), :] = pair_in[:half, :].astype(F32)
    xt[rblock(z), :LANES] = own_f[...].astype(BF16)
    for q in range(3):
        over_far(q).start()
    for j in range(3):
        over_near(3, j).start()
    send_over_x(z)

    @pl.when(first)
    def _():
        remote(give_dn, wt.at[:LANES, :], s_pair.at[1], r_pair.at[1], partner).start()

    @pl.when(c == 1)
    def _():
        remote(give_up, w.at[:, LANES:], s_pair.at[2], r_pair.at[2], partner).start()

    def take_near(q, j):
        zz = back_by(far[q] + near[j])
        remote(block(zz), block(zz), s_near.at[q, j], r_near.at[q, j], at_z(1)).wait_recv()
        send_over_x(zz)

    @pl.when(first)
    def _():
        w[:, :LANES] = give_up[...]
        remote(give_up, w.at[:, LANES:], s_pair.at[1], r_pair.at[2], partner).wait_recv()

        def turn(i):
            tall = pl.ds(pl.multiple_of(i * LANES, LANES), LANES)
            wt[:, tall] = w[tall, :].T
        loop(width // LANES, turn)

    @pl.when(c == 1)
    def _():
        wt[LANES:, :] = give_dn[...]
        remote(give_dn, wt.at[:LANES, :], s_pair.at[2], r_pair.at[1], partner).wait_recv()

        def turn(i):
            tall = pl.ds(pl.multiple_of(i * LANES, LANES), LANES)
            w[tall, :] = wt[:, tall].T
        loop(width // LANES, turn)

    take_near(3, 1)
    take_near(3, 2)
    for q in (1, 2, 0):
        zz = back_by(far[q])
        remote(block(zz), block(zz), s_far.at[q], r_far.at[q], at_z(1)).wait_recv()
        for j in range(3):
            over_near(q, j).start()
        send_over_x(zz)
    take_near(3, 0)
    for q in (1, 2, 0):
        for j in (1, 2, 0):
            take_near(q, j)

    chunks = ((0, 1), (1, 2), (3, 1))

    def lanes(ch):
        return pl.ds(chunks[ch][0] * LANES, chunks[ch][1] * LANES)

    def hblock(i):
        return pl.ds(pl.multiple_of(i * hrows, 16), hrows)

    y_order = sorted(range(1, ny), key=lambda k: -min(k, ny - k))

    def share_of(ch, k):
        return remote(part_b.at[hblock(lax.rem(y + k, ny)), lanes(ch)], got_b.at[k, :, lanes(ch)],
                      s_b.at[ch, k], r_b.at[ch, k], at_y(k))

    def swap(ch):
        return remote(share.at[:, lanes(ch)], other.at[:, lanes(ch)], s_swap.at[ch], r_swap.at[ch], partner)

    def spread(ch, k):
        rows_of = ht.at[hblock(y), lanes(ch)]
        return remote(rows_of, rows_of, s_h.at[ch, k], r_h.at[ch, k], at_y(k))

    def first_product(ch):
        for i in range(chunks[ch][0], sum(chunks[ch])):
            cols = slice(i * LANES, (i + 1) * LANES)
            p = dot(wt[...], xt[:, cols])
            part_f[:, cols] = p
            part_b[:, cols] = p.astype(BF16)
        for k in y_order:
            share_of(ch, k).start()

    def add_shares(ch):
        total = part_f[hblock(y), lanes(ch)]
        for k in reversed(y_order):
            share_of(ch, k).wait_recv()
            total = total + got_b[k, :, lanes(ch)].astype(F32)
        share[:, lanes(ch)] = total
        swap(ch).start()

    def activate(ch):
        swap(ch).wait_recv()
        mine, theirs = share[:, lanes(ch)], other[:, lanes(ch)]
        pre = jnp.where(first, mine, theirs)
        cdf = 0.5 * (1.0 + lax.erf(pre * (1.0 / math.sqrt(2.0))))
        dens = jnp.exp(-0.5 * pre * pre) * (1.0 / math.sqrt(2.0 * math.pi))
        made = jnp.where(first, theirs * (cdf + pre * dens), pre * cdf)
        ht[hblock(y), lanes(ch)] = made.astype(BF16)
        for k in y_order:
            spread(ch, k).start()

    def gathered(ch):
        for k in reversed(y_order):
            landing = ht.at[hblock(lax.rem(y + ny - k, ny)), lanes(ch)]
            remote(landing, landing, s_h.at[ch, k], r_h.at[ch, k], at_y(1)).wait_recv()

    def arrived(i):
        for k in range(1, nx):
            landing = block(i, place[(nx - k) % nx])
            remote(landing, landing, s_ax.at[k, i], r_ax.at[k, i], at_x(1)).wait_recv()

    first_product(0)
    add_shares(0)
    activate(0)
    loop(nz, arrived)
    first_product(1)
    first_product(2)
    add_shares(1)
    activate(1)
    add_shares(2)
    activate(2)

    def to_x(k, d):
        at = place[k] * LANES
        return remote(send_c.at[rblock(d), at:at + LANES], got_x.at[k, rblock(d), :],
                      s_cx.at[k, d], r_cx.at[k, d], at_x(k))

    def second_product(ch):
        def one(i):
            d = lax.rem(z + far_first(i), nz)
            send_c[rblock(d), lanes(ch)] = dot(w[rblock(d), :], ht[:, lanes(ch)]).astype(BF16)
            for at in range(chunks[ch][0], sum(chunks[ch])):
                to_x(order[at], d).start()
        loop(nz, one)

    def own_product(i):
        tall = pl.ds(pl.multiple_of(i * 2 * LANES, 2 * LANES), 2 * LANES)
        own_c[tall, :] = dot(w[tall, :], ht[:, :LANES])

    gathered(0)
    loop(width // (2 * LANES), own_product)
    gathered(1)
    second_product(1)
    gathered(2)
    second_product(2)

    step_rows = 2 * LANES

    @pl.when(first)
    def _():
        def grad(i):
            tall = pl.ds(pl.multiple_of(i * step_rows, step_rows), step_rows)
            p = dot(xt[tall, :], ht[...], ((1,), (1,))).astype(BF16)
            o_gu[tall, :] = p[:, :fcols]
            g_give_up[tall, :] = p[:, LANES:]
        loop(width // step_rows, grad)
        remote(g_give_up, g_got_up, s_pair.at[4], r_pair.at[4], partner).start()

    @pl.when(c == 1)
    def _():
        def grad(i):
            tall = pl.ds(pl.multiple_of(i * step_rows, step_rows), step_rows)
            p = dot(ht[...], xt[tall, :], ((1,), (1,))).astype(BF16)
            g_give_dn[:, tall] = p[:LANES, :]
            o_gd[:, tall] = p[LANES:LANES + fcols, :]
        loop(width // step_rows, grad)
        remote(g_give_dn, g_got_dn, s_pair.at[5], r_pair.at[5], partner).start()

    def to_z(k):
        d = lax.rem(z + k, nz)
        return remote(send_z.at[rblock(d), :], got_z.at[z], s_cz.at[k], r_cz.at[z], at_z(k))

    def add_x(d):
        total = own_c[rblock(d), :]
        for k in range(1, nx):
            to_x(k, d).wait_recv()
            total = total + got_x[k, rblock(d), :].astype(F32)
        return total

    def pass_on(i):
        k = far_first(i)
        d = lax.rem(z + k, nz)
        send_z[rblock(d), :] = add_x(d).astype(BF16)
        to_z(k).start()
    loop(nz - 1, pass_on)
    final[:rows, :] = add_x(z)

    def collect(i):
        s = lax.rem(z + far_first(nz - 2 - i), nz)
        remote(got_z.at[s], got_z.at[s], s_cz.at[1], r_cz.at[s], at_z(1)).wait_recv()
        final[:rows, :] += got_z[s].astype(F32)
    loop(nz - 1, collect)

    out_give[...] = jnp.zeros_like(out_give)
    out_give[:half, :] = final[pl.ds(pl.multiple_of((1 - c) * half, 8), half), :].astype(BF16)
    back = remote(out_give, out_got, s_pair.at[6], r_pair.at[6], partner)
    back.start()
    kept = final[pl.ds(pl.multiple_of(c * half, 8), half), :].astype(BF16)

    @pl.when(first)
    def _():
        remote(g_give_dn, g_got_dn, s_pair.at[4], r_pair.at[5], partner).wait_recv()
        o_gd[...] = g_got_dn[:fcols, :]
        o_gt[...] = kept
        back.wait_recv()
        o_out[...] = out_got[:half, :]
        remote(give_dn, wt.at[:LANES, :], s_pair.at[1], r_pair.at[1], partner).wait_send()
        remote(g_give_up, g_got_up, s_pair.at[4], r_pair.at[4], partner).wait_send()

    @pl.when(c == 1)
    def _():
        remote(g_give_up, g_got_up, s_pair.at[5], r_pair.at[4], partner).wait_recv()
        o_gu[...] = g_got_up[:, :fcols]
        o_out[...] = kept
        back.wait_recv()
        o_gt[...] = out_got[:half, :]
        remote(give_up, w.at[:, LANES:], s_pair.at[2], r_pair.at[2], partner).wait_send()
        remote(g_give_dn, g_got_dn, s_pair.at[5], r_pair.at[5], partner).wait_send()

    to_pair.wait_send()
    back.wait_send()
    for ch in range(len(chunks)):
        swap(ch).wait_send()
        for k in y_order:
            share_of(ch, k).wait_send()
            spread(ch, k).wait_send()
    for q in range(4):
        if q < 3:
            over_far(q).wait_send()
        for j in range(3):
            over_near(q, j).wait_send()
    loop(nz - 1, lambda i: to_z(far_first(i)).wait_send())

    def sent(i):
        for k in range(1, nx):
            over_x(k, i).wait_send()
            to_x(k, i).wait_send()
    loop(nz, sent)


def local(shape, tokens, w_up, w_down, out_grad):
    tokens, out_grad = tokens.T, out_grad.T
    nx, ny, nz = shape["gy"], shape["gx"], shape["gz"] // 2
    half = tokens.shape[0]
    rows, padded = 2 * half, -(-half // 16) * 16
    width, fcols = w_up.shape
    count = tokens.shape[1] * nx
    hid = 2 * LANES
    vmem, dma = pltpu.VMEM, pltpu.SemaphoreType.DMA
    scratch = [
        vmem((padded, LANES), BF16), vmem((padded, LANES), BF16), vmem((rows, LANES), F32),
        vmem((width, count), BF16), vmem((width, hid), BF16), vmem((hid, width), BF16),
        vmem((width, LANES), BF16), vmem((LANES, width), BF16),
        vmem((hid, count), F32), vmem((hid, count), BF16), vmem((ny, hid // ny, count), BF16),
        vmem((hid // ny, count), F32), vmem((hid // ny, count), F32), vmem((hid, count), BF16),
        vmem((width, count), BF16), vmem((nx, width, LANES), BF16), vmem((width, LANES), F32),
        vmem((width, LANES), BF16), vmem((nz, rows, LANES), BF16), vmem((rows, LANES), F32),
        vmem((padded, LANES), BF16), vmem((padded, LANES), BF16),
        vmem((width, LANES), BF16), vmem((LANES, width), BF16),
        vmem((width, LANES), BF16), vmem((LANES, width), BF16),
        dma((7,)), dma((7,)), dma((3,)), dma((3,)), dma((4, 3)), dma((4, 3)),
        dma((nx, nz)), dma((nx, nz)),
        dma((3,)), dma((3,)), dma((3, ny)), dma((3, ny)), dma((3, ny)), dma((3, ny)),
        dma((nx, nz)), dma((nx, nz)), dma((nz,)), dma((nz,)),
    ]
    whole = pl.BlockSpec(memory_space=pltpu.VMEM)
    out, grad_tokens, grad_up, grad_down = pl.pallas_call(
        functools.partial(kernel, (nx, ny, nz, rows, half, fcols)),
        out_shape=(
            jax.ShapeDtypeStruct(tokens.shape, BF16), jax.ShapeDtypeStruct(tokens.shape, BF16),
            jax.ShapeDtypeStruct(w_up.shape, BF16), jax.ShapeDtypeStruct(w_down.shape, BF16)),
        in_specs=[whole] * 4,
        out_specs=(whole,) * 4,
        scratch_shapes=scratch,
        compiler_params=pltpu.CompilerParams(
            collective_id=0, has_side_effects=True, vmem_limit_bytes=48 * 1024 * 1024),
    )(tokens, out_grad, w_up, w_down)
    return out.T, grad_tokens.T, grad_up, grad_down


def solution(mesh):
    tokens, up, down = P("gy", ("gx", "gz")), P("gx", ("gz", "gy")), P(("gz", "gy"), "gx")
    return jax.shard_map(
        functools.partial(local, dict(mesh.shape)),
        mesh=mesh,
        in_specs=(tokens, up, down, tokens),
        out_specs=(tokens, tokens, up, down),
        check_vma=False,
    )
```

time: 107 us -> 97.3 us (0.909)
  Pallas kernels: 101 us -> 90.3 us
    pallas_call x1, Pallas kernels: 101 us -> 90.3 us  [local(): pl.pallas_call(functools.partial(kernel, (nx, ny, nz, rows, half, fcols))...]
    unnamed x10 -> x12, local copies, waits for them, and re-layouts: 4.34 us -> 5.99 us
    pallas_call x2 -> x0, local copies, waits for them, and re-layouts: 1.37 us -> none  [local(): pl.pallas_call(functools.partial(kernel, (nx, ny, nz, rows, half, fcols))...]
where the time goes in v2:
time: 97.3 us; the launch traced here: 97 us
  Pallas kernels  90.3 us (93%)
  local copies, waits for them, and re-layouts  5.99 us (6%)
    pallas_call x1, Pallas kernels, local(): pl.pallas_call(functools.partial(kernel, (nx, ny, nz, rows, half, fcols))...  90.3 us
    unnamed x12, local copies, waits for them, and re-layouts  5.99 us

profile of v2, /device:TPU:1, one launch (start us, length us, event | category | flops | bytes accessed | tf_op | source)
XLA Modules:
  0.0 97.0 jit_solution(15337101242608576738)
XLA Ops:
  0.6 0.0 copy-start
  0.6 1.0 copy-done
  1.6 0.0 copy-start.1
  1.6 1.0 %copy-done.1 = bf16[124,1280]{1,0:T(8,128)(2,1)S(1)} copy-done((bf16[124,1280]{1,0:T(8,128)(2,1)S(1)}, bf16[124,1280]{1,0:T(8,128)(2,1)}, u32[]{:S(2)}) %copy-start.1) | copy-done | bytes 317464
  2.6 0.0 copy-start.2
  2.6 0.7 copy-done.2
  3.3 0.0 copy-start.3
  3.3 0.7 copy-done.3
  4.0 90.3 %shard_map.75 = (bf16[40,128]{1,0:T(8,128)(2,1)S(1)}, bf16[40,128]{1,0:T(8,128)(2,1)S(1)}, bf16[1280,124]{1,0:T(8,128)(2,1)S(1)}, bf16[124,1280]{1,0:T(8,128)(2,1)S(1)}) custom-call(bf16[40,128]{1,0:T(8,128)(2,1)S(1)} %bitcast.6, bf16[40,128]{1,0:T(8,128)(2,1)S(1)} %bitcast.7, bf16[1280,124]{1,0:T(8,128)(2,1)S(1)} %copy-done, bf16[124,1280]{1,0:T(8,128)(2,1)S(1)} %copy-done.1), custom_call_target="tpu_custom_call" | custom-call | tf_op jit(solution)/shard_map/pallas_call | solution.py:388
  94.3 0.6 copy.12
  94.9 0.6 copy.13
  95.5 0.7 copy.14
  96.2 0.7 copy.15
Async XLA Ops:
  0.6 1.0 %copy-start = (bf16[1280,124]{1,0:T(8,128)(2,1)S(1)}, bf16[1280,124]{1,0:T(8,128)(2,1)}, u32[]{:S(2)}) copy-start(bf16[1280,124]{1,0:T(8,128)(2,1)} %refs_2_.1) | copy-start | bytes 952324
  1.6 1.0 %copy-start.1 = (bf16[124,1280]{1,0:T(8,128)(2,1)S(1)}, bf16[124,1280]{1,0:T(8,128)(2,1)}, u32[]{:S(2)}) copy-start(bf16[124,1280]{1,0:T(8,128)(2,1)} %refs_3_.1) | copy-start | bytes 952324
  2.6 0.7 copy-start.2
  3.3 0.7 copy-start.3

commit v3 on v2

--- a/solution.py
+++ b/solution.py
@@ -19,12 +19,12 @@
 
 def kernel(sizes, *refs):
     nx, ny, nz, rows, half, fcols = sizes
-    (tok, cot, w_up, w_dn, o_out, o_gt, o_gu, o_gd,
-     give, pair_in, own_f, xt, w, wt, give_up, give_dn,
+    (tok, cot, up_hbm, w_dn, o_out, o_gt, o_gu, o_gd,
+     w_up, give, pair_in, own_f, xt, w, wt, give_up, give_dn,
      part_f, part_b, got_b, share, other, ht,
-     send_c, got_x, own_c, send_z, got_z, final, out_give, out_got,
+     send_c, got_x, own_c, send_z, got_near, got_far, final, out_give, out_got,
      g_give_up, g_give_dn, g_got_up, g_got_dn,
-     s_pair, r_pair, s_far, r_far, s_near, r_near, s_ax, r_ax, s_swap, r_swap, s_b, r_b, s_h, r_h, s_cx, r_cx, s_cz, r_cz) = refs
+     s_in, s_pair, r_pair, s_far, r_far, s_near, r_near, s_ax, r_ax, s_swap, r_swap, s_b, r_b, s_h, r_h, s_cx, r_cx, s_cn, r_cn, s_cf, r_cf) = refs
     y, x = lax.axis_index("gx"), lax.axis_index("gy")
     g = lax.axis_index("gz")
     z, c = lax.div(g, 2), lax.rem(g, 2)
@@ -57,22 +57,20 @@
             return carry
         lax.fori_loop(0, n, step, 0)
 
-    def far_first(i):
-        m = lax.div(i + 1, 2)
-        return nz // 2 + m * (2 * lax.rem(i + 1, 2) - 1)
-
     def rblock(i):
         return pl.ds(pl.multiple_of(i * rows, 16), rows)
 
-    def lblock(i):
-        return pl.ds(pl.multiple_of(i * LANES, LANES), LANES)
+    load = pltpu.make_async_copy(up_hbm, w_up, s_in.at[0])
+    load.start()
 
     barrier = pltpu.get_barrier_semaphore()
 
     def hello(device):
         pl.semaphore_signal(barrier, inc=1, device_id=device, device_id_type=MESH)
 
-    loop(nz - 1, lambda i: hello(at_z(far_first(i))))
+    z_peers = (nz // 2, nz // 4, 3 * nz // 4, 2, nz - 2, 1, nz - 1)
+    for k in z_peers:
+        hello(at_z(k))
     for k in range(1, ny):
         hello(at_y(k))
     for k in range(1, nx):
@@ -80,13 +78,11 @@
     hello(partner)
 
     first = c == 0
+    give_dn[...] = jnp.zeros_like(give_dn)
+    give_up[...] = jnp.zeros_like(give_up)
     give[...] = jnp.zeros_like(give)
     give[:half, :] = jnp.where(first, cot[...], tok[...])
     own_f[pl.ds(pl.multiple_of(c * half, 8), half), :] = jnp.where(first, tok[...], cot[...]).astype(F32)
-    give_dn[...] = jnp.zeros_like(give_dn)
-    give_up[...] = jnp.zeros_like(give_up)
-    give_dn[:fcols, :] = w_dn[...]
-    give_up[:, :fcols] = w_up[...]
 
     order = (0, 2, 1, 3)
     place = {k: at for at, k in enumerate(order)}
@@ -114,7 +110,7 @@
         for k in (2, 1, 3):
             over_x(k, zz).start()
 
-    pl.semaphore_wait(barrier, 1 + (nz - 1) + (nx - 1) + (ny - 1))
+    pl.semaphore_wait(barrier, 1 + len(z_peers) + (nx - 1) + (ny - 1))
     to_pair.start()
     to_pair.wait_recv()
     own_f[pl.ds(pl.multiple_of((1 - c) * half, 8), half), :] = pair_in[:half, :].astype(F32)
@@ -124,6 +120,10 @@
     for j in range(3):
         over_near(3, j).start()
     send_over_x(z)
+
+    load.wait()
+    give_dn[:fcols, :] = w_dn[...]
+    give_up[:, :fcols] = w_up[...]
 
     @pl.when(first)
     def _():
@@ -241,25 +241,30 @@
     add_shares(2)
     activate(2)
 
-    def to_x(k, d):
-        at = place[k] * LANES
-        return remote(send_c.at[rblock(d), at:at + LANES], got_x.at[k, rblock(d), :],
-                      s_cx.at[k, d], r_cx.at[k, d], at_x(k))
+    hops = near + (0,)
+    group = len(hops) * rows
+
+    def slot(q, n):
+        return pl.ds((q * len(hops) + n) * rows, rows)
+
+    def goal(q, n):
+        return lax.rem(z + far[q] + hops[n], nz)
+
+    def to_x(k, q):
+        at, tall = place[k] * LANES, pl.ds(q * group, group)
+        return remote(send_c.at[tall, at:at + LANES], got_x.at[k, tall, :], s_cx.at[k, q], r_cx.at[k, q], at_x(k))
 
     def second_product(ch):
-        def one(i):
-            d = lax.rem(z + far_first(i), nz)
-            send_c[rblock(d), lanes(ch)] = dot(w[rblock(d), :], ht[:, lanes(ch)]).astype(BF16)
+        for q in range(4):
+            for n in range(4):
+                send_c[slot(q, n), lanes(ch)] = dot(w[rblock(goal(q, n)), :], ht[:, lanes(ch)]).astype(BF16)
             for at in range(chunks[ch][0], sum(chunks[ch])):
-                to_x(order[at], d).start()
-        loop(nz, one)
-
-    def own_product(i):
-        tall = pl.ds(pl.multiple_of(i * 2 * LANES, 2 * LANES), 2 * LANES)
-        own_c[tall, :] = dot(w[tall, :], ht[:, :LANES])
+                to_x(order[at], q).start()
 
     gathered(0)
-    loop(width // (2 * LANES), own_product)
+    for q in range(4):
+        for n in range(4):
+            own_c[slot(q, n), :] = dot(w[rblock(goal(q, n)), :], ht[:, :LANES])
     gathered(1)
     second_product(1)
     gathered(2)
@@ -287,30 +292,47 @@
         loop(width // step_rows, grad)
         remote(g_give_dn, g_got_dn, s_pair.at[5], r_pair.at[5], partner).start()
 
-    def to_z(k):
-        d = lax.rem(z + k, nz)
-        return remote(send_z.at[rblock(d), :], got_z.at[z], s_cz.at[k], r_cz.at[z], at_z(k))
-
-    def add_x(d):
-        total = own_c[rblock(d), :]
+    def to_near(q, n):
+        return remote(send_z.at[slot(q, n), :], got_near.at[q, n], s_cn.at[q, n], r_cn.at[q, n], at_z(hops[n]))
+
+    def to_far(q):
+        return remote(send_z.at[slot(q, 3), :], got_far.at[q], s_cf.at[q], r_cf.at[q], at_z(far[q]))
+
+    def add_x(q):
         for k in range(1, nx):
-            to_x(k, d).wait_recv()
-            total = total + got_x[k, rblock(d), :].astype(F32)
+            to_x(k, q).wait_recv()
+        for n in range(4):
+            total = own_c[slot(q, n), :]
+            for k in range(1, nx):
+                total = total + got_x[k, slot(q, n), :].astype(F32)
+            if n < 3:
+                send_z[slot(q, n), :] = total.astype(BF16)
+                to_near(q, n).start()
+            else:
+                own_c[slot(q, n), :] = total
+
+    def add_near(q):
+        total = own_c[slot(q, 3), :]
+        for n in range(3):
+            to_near(q, n).wait_recv()
+            total = total + got_near[q, n].astype(F32)
+        if q < 3:
+            send_z[slot(q, 3), :] = total.astype(BF16)
+            to_far(q).start()
         return total
 
-    def pass_on(i):
-        k = far_first(i)
-        d = lax.rem(z + k, nz)
-        send_z[rblock(d), :] = add_x(d).astype(BF16)
-        to_z(k).start()
-    loop(nz - 1, pass_on)
-    final[:rows, :] = add_x(z)
-
-    def collect(i):
-        s = lax.rem(z + far_first(nz - 2 - i), nz)
-        remote(got_z.at[s], got_z.at[s], s_cz.at[1], r_cz.at[s], at_z(1)).wait_recv()
-        final[:rows, :] += got_z[s].astype(F32)
-    loop(nz - 1, collect)
+    add_x(0)
+    add_x(1)
+    add_near(0)
+    add_x(2)
+    add_near(1)
+    add_x(3)
+    add_near(2)
+    total = add_near(3)
+    for q in (1, 2, 0):
+        to_far(q).wait_recv()
+        total = total + got_far[q].astype(F32)
+    final[...] = total
 
     out_give[...] = jnp.zeros_like(out_give)
     out_give[:half, :] = final[pl.ds(pl.multiple_of((1 - c) * half, 8), half), :].astype(BF16)
@@ -350,12 +372,17 @@
             over_far(q).wait_send()
         for j in range(3):
             over_near(q, j).wait_send()
-    loop(nz - 1, lambda i: to_z(far_first(i)).wait_send())
+    for q in range(4):
+        if q < 3:
+            to_far(q).wait_send()
+        for n in range(3):
+            to_near(q, n).wait_send()
+        for k in range(1, nx):
+            to_x(k, q).wait_send()
 
     def sent(i):
         for k in range(1, nx):
             over_x(k, i).wait_send()
-            to_x(k, i).wait_send()
     loop(nz, sent)
 
 
@@ -369,20 +396,21 @@
     hid = 2 * LANES
     vmem, dma = pltpu.VMEM, pltpu.SemaphoreType.DMA
     scratch = [
+        vmem(w_up.shape, BF16),
         vmem((padded, LANES), BF16), vmem((padded, LANES), BF16), vmem((rows, LANES), F32),
         vmem((width, count), BF16), vmem((width, hid), BF16), vmem((hid, width), BF16),
         vmem((width, LANES), BF16), vmem((LANES, width), BF16),
         vmem((hid, count), F32), vmem((hid, count), BF16), vmem((ny, hid // ny, count), BF16),
         vmem((hid // ny, count), F32), vmem((hid // ny, count), F32), vmem((hid, count), BF16),
         vmem((width, count), BF16), vmem((nx, width, LANES), BF16), vmem((width, LANES), F32),
-        vmem((width, LANES), BF16), vmem((nz, rows, LANES), BF16), vmem((rows, LANES), F32),
+        vmem((width, LANES), BF16), vmem((4, 3, rows, LANES), BF16), vmem((3, rows, LANES), BF16), vmem((rows, LANES), F32),
         vmem((padded, LANES), BF16), vmem((padded, LANES), BF16),
         vmem((width, LANES), BF16), vmem((LANES, width), BF16),
         vmem((width, LANES), BF16), vmem((LANES, width), BF16),
-        dma((7,)), dma((7,)), dma((3,)), dma((3,)), dma((4, 3)), dma((4, 3)),
+        dma((1,)), dma((7,)), dma((7,)), dma((3,)), dma((3,)), dma((4, 3)), dma((4, 3)),
         dma((nx, nz)), dma((nx, nz)),
         dma((3,)), dma((3,)), dma((3, ny)), dma((3, ny)), dma((3, ny)), dma((3, ny)),
-        dma((nx, nz)), dma((nx, nz)), dma((nz,)), dma((nz,)),
+        dma((nx, 4)), dma((nx, 4)), dma((4, 3)), dma((4, 3)), dma((3,)), dma((3,)),
     ]
     whole = pl.BlockSpec(memory_space=pltpu.VMEM)
     out, grad_tokens, grad_up, grad_down = pl.pallas_call(
@@ -390,7 +418,7 @@
         out_shape=(
             jax.ShapeDtypeStruct(tokens.shape, BF16), jax.ShapeDtypeStruct(tokens.shape, BF16),
             jax.ShapeDtypeStruct(w_up.shape, BF16), jax.ShapeDtypeStruct(w_down.shape, BF16)),
-        in_specs=[whole] * 4,
+        in_specs=[whole, whole, pl.BlockSpec(memory_space=pltpu.HBM), whole],
         out_specs=(whole,) * 4,
         scratch_shapes=scratch,
         compiler_params=pltpu.CompilerParams(

time: 97.3 us -> 95.3 us (0.979)
  Pallas kernels: 90.3 us -> 88.4 us
    pallas_call x1, Pallas kernels: 90.3 us -> 88.4 us  [local(): pl.pallas_call(functools.partial(kernel, (nx, ny, nz, rows, half, fcols))...]
where the time goes in v3:
time: 95.3 us; the launch traced here: 95 us
  Pallas kernels  88.4 us (93%)
  local copies, waits for them, and re-layouts  5.99 us (6%)
    pallas_call x1, Pallas kernels, local(): pl.pallas_call(functools.partial(kernel, (nx, ny, nz, rows, half, fcols))...  88.4 us
    unnamed x12, local copies, waits for them, and re-layouts  5.99 us

profile of v3, /device:TPU:1, one launch (start us, length us, event | category | flops | bytes accessed | tf_op | source)
XLA Modules:
  0.0 95.0 jit_solution(13532603899305278839)
XLA Ops:
  0.6 0.0 copy-start
  0.6 1.0 %copy-done = bf16[1280,124]{1,0:T(8,128)(2,1)S(1)} copy-done((bf16[1280,124]{1,0:T(8,128)(2,1)S(1)}, bf16[1280,124]{1,0:T(8,128)(2,1)}, u32[]{:S(2)}) %copy-start) | copy-done | bytes 317464
  1.6 0.0 copy-start.1
  1.6 1.0 %copy-done.1 = bf16[124,1280]{1,0:T(8,128)(2,1)S(1)} copy-done((bf16[124,1280]{1,0:T(8,128)(2,1)S(1)}, bf16[124,1280]{1,0:T(8,128)(2,1)}, u32[]{:S(2)}) %copy-start.1) | copy-done | bytes 317464
  2.6 0.0 copy-start.2
  2.6 0.7 copy-done.2
  3.3 0.0 copy-start.3
  3.3 0.7 copy-done.3
  4.0 88.4 %shard_map.75 = (bf16[40,128]{1,0:T(8,128)(2,1)S(1)}, bf16[40,128]{1,0:T(8,128)(2,1)S(1)}, bf16[1280,124]{1,0:T(8,128)(2,1)S(1)}, bf16[124,1280]{1,0:T(8,128)(2,1)S(1)}) custom-call(bf16[40,128]{1,0:T(8,128)(2,1)S(1)} %bitcast.6, bf16[40,128]{1,0:T(8,128)(2,1)S(1)} %bitcast.7, bf16[1280,124]{1,0:T(8,128)(2,1)S(1)} %copy-done, bf16[124,1280]{1,0:T(8,128)(2,1)S(1)} %copy-done.1), custom_call_target="tpu_custom_call" | custom-call | tf_op jit(solution)/shard_map/pallas_call | solution.py:416
  92.4 0.6 copy.12
  93.0 0.6 copy.13
  93.6 0.7 copy.14
  94.3 0.7 copy.15
Async XLA Ops:
  0.6 1.0 %copy-start = (bf16[1280,124]{1,0:T(8,128)(2,1)S(1)}, bf16[1280,124]{1,0:T(8,128)(2,1)}, u32[]{:S(2)}) copy-start(bf16[1280,124]{1,0:T(8,128)(2,1)} %refs_2_.1) | copy-start | bytes 952324
  1.6 1.0 %copy-start.1 = (bf16[124,1280]{1,0:T(8,128)(2,1)S(1)}, bf16[124,1280]{1,0:T(8,128)(2,1)}, u32[]{:S(2)}) copy-start(bf16[124,1280]{1,0:T(8,128)(2,1)} %refs_3_.1) | copy-start | bytes 952324
  2.6 0.7 copy-start.2
  3.3 0.7 copy-start.3

commit v4 on v3

--- a/solution.py
+++ b/solution.py
@@ -270,28 +270,6 @@
     gathered(2)
     second_product(2)
 
-    step_rows = 2 * LANES
-
-    @pl.when(first)
-    def _():
-        def grad(i):
-            tall = pl.ds(pl.multiple_of(i * step_rows, step_rows), step_rows)
-            p = dot(xt[tall, :], ht[...], ((1,), (1,))).astype(BF16)
-            o_gu[tall, :] = p[:, :fcols]
-            g_give_up[tall, :] = p[:, LANES:]
-        loop(width // step_rows, grad)
-        remote(g_give_up, g_got_up, s_pair.at[4], r_pair.at[4], partner).start()
-
-    @pl.when(c == 1)
-    def _():
-        def grad(i):
-            tall = pl.ds(pl.multiple_of(i * step_rows, step_rows), step_rows)
-            p = dot(ht[...], xt[tall, :], ((1,), (1,))).astype(BF16)
-            g_give_dn[:, tall] = p[:LANES, :]
-            o_gd[:, tall] = p[LANES:LANES + fcols, :]
-        loop(width // step_rows, grad)
-        remote(g_give_dn, g_got_dn, s_pair.at[5], r_pair.at[5], partner).start()
-
     def to_near(q, n):
         return remote(send_z.at[slot(q, n), :], got_near.at[q, n], s_cn.at[q, n], r_cn.at[q, n], at_z(hops[n]))
 
@@ -328,6 +306,29 @@
     add_near(1)
     add_x(3)
     add_near(2)
+
+    step_rows = 2 * LANES
+
+    @pl.when(first)
+    def _():
+        def grad(i):
+            tall = pl.ds(pl.multiple_of(i * step_rows, step_rows), step_rows)
+            p = dot(xt[tall, :], ht[...], ((1,), (1,))).astype(BF16)
+            o_gu[tall, :] = p[:, :fcols]
+            g_give_up[tall, :] = p[:, LANES:]
+        loop(width // step_rows, grad)
+        remote(g_give_up, g_got_up, s_pair.at[4], r_pair.at[4], partner).start()
+
+    @pl.when(c == 1)
+    def _():
+        def grad(i):
+            tall = pl.ds(pl.multiple_of(i * step_rows, step_rows), step_rows)
+            p = dot(ht[...], xt[tall, :], ((1,), (1,))).astype(BF16)
+            g_give_dn[:, tall] = p[:LANES, :]
+            o_gd[:, tall] = p[LANES:LANES + fcols, :]
+        loop(width // step_rows, grad)
+        remote(g_give_dn, g_got_dn, s_pair.at[5], r_pair.at[5], partner).start()
+
     total = add_near(3)
     for q in (1, 2, 0):
         to_far(q).wait_recv()

time: 95.3 us -> 95.3 us (level)
  no operation moved by 1% of the time
where the time goes in v4:
time: 95.3 us; the launch traced here: 95 us
  Pallas kernels  88.4 us (93%)
  local copies, waits for them, and re-layouts  5.99 us (6%)
    pallas_call x1, Pallas kernels, local(): pl.pallas_call(functools.partial(kernel, (nx, ny, nz, rows, half, fcols))...  88.4 us
    unnamed x12, local copies, waits for them, and re-layouts  5.99 us

profile of v4, /device:TPU:1, one launch (start us, length us, event | category | flops | bytes accessed | tf_op | source)
XLA Modules:
  0.0 95.0 jit_solution(9022178232271784506)
XLA Ops:
  0.6 0.0 copy-start
  0.6 1.0 %copy-done = bf16[1280,124]{1,0:T(8,128)(2,1)S(1)} copy-done((bf16[1280,124]{1,0:T(8,128)(2,1)S(1)}, bf16[1280,124]{1,0:T(8,128)(2,1)}, u32[]{:S(2)}) %copy-start) | copy-done | bytes 317464
  1.6 0.0 copy-start.1
  1.6 1.0 %copy-done.1 = bf16[124,1280]{1,0:T(8,128)(2,1)S(1)} copy-done((bf16[124,1280]{1,0:T(8,128)(2,1)S(1)}, bf16[124,1280]{1,0:T(8,128)(2,1)}, u32[]{:S(2)}) %copy-start.1) | copy-done | bytes 317464
  2.6 0.0 copy-start.2
  2.6 0.7 copy-done.2
  3.3 0.0 copy-start.3
  3.3 0.7 copy-done.3
  4.0 88.4 %shard_map.75 = (bf16[40,128]{1,0:T(8,128)(2,1)S(1)}, bf16[40,128]{1,0:T(8,128)(2,1)S(1)}, bf16[1280,124]{1,0:T(8,128)(2,1)S(1)}, bf16[124,1280]{1,0:T(8,128)(2,1)S(1)}) custom-call(bf16[40,128]{1,0:T(8,128)(2,1)S(1)} %bitcast.6, bf16[40,128]{1,0:T(8,128)(2,1)S(1)} %bitcast.7, bf16[1280,124]{1,0:T(8,128)(2,1)S(1)} %copy-done, bf16[124,1280]{1,0:T(8,128)(2,1)S(1)} %copy-done.1), custom_call_target="tpu_custom_call" | custom-call | tf_op jit(solution)/shard_map/pallas_call | solution.py:417
  92.4 0.6 copy.12
  93.0 0.6 copy.13
  93.6 0.7 copy.14
  94.3 0.7 copy.15
Async XLA Ops:
  0.6 1.0 %copy-start = (bf16[1280,124]{1,0:T(8,128)(2,1)S(1)}, bf16[1280,124]{1,0:T(8,128)(2,1)}, u32[]{:S(2)}) copy-start(bf16[1280,124]{1,0:T(8,128)(2,1)} %refs_2_.1) | copy-start | bytes 952324
  1.6 1.0 %copy-start.1 = (bf16[124,1280]{1,0:T(8,128)(2,1)S(1)}, bf16[124,1280]{1,0:T(8,128)(2,1)}, u32[]{:S(2)}) copy-start(bf16[124,1280]{1,0:T(8,128)(2,1)} %refs_3_.1) | copy-start | bytes 952324
  2.6 0.7 copy-start.2
  3.3 0.7 copy-start.3
